TPU v7x, 256 devices: a whole 4x4x8 slice. The times are simulated.
256 devices in a mesh: px: 32 (over x, y, core), py: 8 (over z).
Axes of the slice: x: 4, y: 4, z: 8, core: 2. Of those that a mesh axis runs over, the one named last changes fastest.
Arguments:
- forcing: float32 [3, 224, 56, 7, 128], P(None, 'px', 'py'), may hold values from -600 to 600
- initial_guess: float32 [3, 224, 56, 7, 128], P(None, 'px', 'py'), may hold values from -3 to 3
- forward_velocity: bfloat16 [3, 224, 56, 7, 128], P(None, 'px', 'py'), may hold values from -4 to 4
- free_mask: int32 [224, 56, 7, 128], P('px', 'py'), may hold values 0 or 1
Outputs:
- adjoint_velocity: float32 [3, 224, 56, 7, 128], P(None, 'px', 'py')
- search_direction: float32 [3, 224, 56, 7, 128], P(None, 'px', 'py')
Inputs may be any that keep to these rules, and one draw needn't show every extreme that they name: `free_mask`: 1 marks a free node, 0 a node held at its initial guess.
All inputs are finite; a program needn't handle non-finite values. No bound on the sum of `free_mask` on one device may be relied on, other than what follows from the above.
Results may differ from a plain program's by a relative error of at most 0.00085.
Values sent between devices are 32-bit elements; how exact they have to be, the bound alone decides.
A program may use at most 64 MiB of HBM per device.

v0:
```python
import jax
import jax.numpy as jnp
import numpy as np
from jax import lax
from jax.sharding import PartitionSpec as P

ITERS = 2
VISC_BASE = 0.5
VISC_GAIN = 0.5
HELMHOLTZ = 20.0


def shifted(value, axis, by):
    count = lax.axis_size(axis)
    return lax.ppermute(value, axis, [(i, (i + by) % count) for i in range(count)])


def passed_along(block, axis, distance):
    devices = range(lax.axis_size(axis))
    route = [(i - distance, i) for i in devices if i - distance in devices]
    return lax.ppermute(block, axis, route)


def gll_tables():
    poly_order = 7
    gll_points = np.array(
        [
            -1.0,
            -0.8717401485096066,
            -0.5917001814331423,
            -0.20929921790247888,
            0.20929921790247888,
            0.5917001814331423,
            0.8717401485096066,
            1.0,
        ]
    )
    previous = np.ones(8)
    legendre = gll_points.copy()
    for degree in range(1, poly_order):
        following = ((2 * degree + 1) * gll_points * legendre - degree * previous) / (degree + 1)
        previous = legendre
        legendre = following
    quad_weights = 2.0 / (poly_order * (poly_order + 1) * legendre**2)
    derivative = np.zeros((8, 8))
    for target in range(8):
        for source in range(8):
            if target != source:
                derivative[target, source] = (
                    legendre[target] / legendre[source] / (gll_points[target] - gll_points[source])
                )
    derivative[0, 0] = -poly_order * (poly_order + 1) / 4.0
    derivative[7, 7] = poly_order * (poly_order + 1) / 4.0
    node_weights = quad_weights[:7].copy()
    node_weights[0] = 2.0 * quad_weights[0]
    return (quad_weights, derivative, node_weights)


def line_weights(length):
    node_weights = gll_tables()[2]
    return jnp.asarray(np.tile(node_weights, length // 7), jnp.float32)


def local_view(values, dimension, elements):
    leading = lax.slice_in_dim(values, 0, 7 * elements, axis=dimension)
    leading = leading.reshape(
        values.shape[:dimension] + (elements, 7) + values.shape[dimension + 1 :]
    )
    closing = lax.slice_in_dim(values, 7, 7 * elements + 1, stride=7, axis=dimension)
    closing = jnp.expand_dims(closing, dimension + 1)
    return jnp.concatenate([leading, closing], axis=dimension + 1)


def fold_view(local_part, dimension, elements):
    leading = lax.slice_in_dim(local_part, 0, 7, axis=dimension + 1)
    out_shape = local_part.shape[:dimension] + (7 * elements,) + local_part.shape[dimension + 2 :]
    leading = leading.reshape(out_shape)
    closing = lax.slice_in_dim(local_part, 7, 8, axis=dimension + 1)
    padding = jnp.zeros(
        closing.shape[: dimension + 1] + (6,) + closing.shape[dimension + 2 :], local_part.dtype
    )
    closing = jnp.concatenate([padding, closing], axis=dimension + 1).reshape(out_shape)
    zero_node = jnp.zeros(
        out_shape[:dimension] + (1,) + out_shape[dimension + 1 :], local_part.dtype
    )
    return jnp.concatenate([leading, zero_node], axis=dimension) + jnp.concatenate(
        [zero_node, closing], axis=dimension
    )


def z_view(values):
    first_layer = values[..., 0:1, :]
    return jnp.concatenate([values, jnp.roll(first_layer, -1, axis=-1)], axis=-2)


def z_fold(local_part):
    first_node = local_part[..., 0:1, :] + jnp.roll(local_part[..., 7:8, :], 1, axis=-1)
    return jnp.concatenate([first_node, local_part[..., 1:7, :]], axis=-2)


def kernel(values, coef_part, trailing):
    quad_weights, derivative, node_weights = gll_tables()
    deriv_table = jnp.asarray(derivative, jnp.float32)
    weight_column = jnp.asarray(quad_weights, jnp.float32).reshape((8,) + (1,) * trailing)
    index_tail = "sab"[3 - trailing :]
    gradient = jnp.einsum(
        "mk,...k" + index_tail + "->...m" + index_tail,
        deriv_table,
        values,
        precision=lax.Precision.HIGHEST,
    )
    flux_term = gradient * (weight_column * coef_part)
    return jnp.einsum(
        "mk,...m" + index_tail + "->...k" + index_tail,
        deriv_table,
        flux_term,
        precision=lax.Precision.HIGHEST,
    )


def diag_kernel(coef_part, trailing):
    quad_weights, derivative, node_weights = gll_tables()
    square_table = jnp.asarray(derivative * derivative, jnp.float32)
    weight_column = jnp.asarray(quad_weights, jnp.float32).reshape((8,) + (1,) * trailing)
    index_tail = "sab"[3 - trailing :]
    return jnp.einsum(
        "mk,...m" + index_tail + "->...k" + index_tail,
        square_table,
        weight_column * coef_part,
        precision=lax.Precision.HIGHEST,
    )


def element_factor():
    return 1.0


def direction_term(values, coef_ext, from_right):
    field_dim = values.ndim - from_right
    coef_dim = coef_ext.ndim - from_right
    elements = (values.shape[field_dim] - 1) // 7
    local_part = kernel(
        local_view(values, field_dim, elements),
        local_view(coef_ext, coef_dim, elements),
        from_right - 1,
    )
    local_part = local_part * element_factor()
    return fold_view(local_part, field_dim, elements)


def diag_term(coef_ext, from_right):
    coef_dim = coef_ext.ndim - from_right
    elements = (coef_ext.shape[coef_dim] - 1) // 7
    local_part = diag_kernel(local_view(coef_ext, coef_dim, elements), from_right - 1)
    local_part = local_part * element_factor()
    return fold_view(local_part, coef_dim, elements)


def extend_x(values):
    dimension = values.ndim - 4
    first_layer = lax.slice_in_dim(values, 0, 1, axis=dimension)
    upper_part = shifted(first_layer, "px", -1)
    return jnp.concatenate([values, upper_part], axis=dimension)


def extend_y(values):
    dimension = values.ndim - 3
    first_layer = lax.slice_in_dim(values, 0, 1, axis=dimension)
    upper_part = passed_along(first_layer, "py", -1)
    return jnp.concatenate([values, upper_part], axis=dimension)


def reduce_x(values):
    dimension = values.ndim - 4
    length = values.shape[dimension]
    last_node = lax.slice_in_dim(values, length - 1, length, axis=dimension)
    arrived = shifted(last_node, "px", 1)
    first_node = lax.slice_in_dim(values, 0, 1, axis=dimension) + arrived
    return jnp.concatenate(
        [first_node, lax.slice_in_dim(values, 1, length - 1, axis=dimension)], axis=dimension
    )


def reduce_y(values):
    dimension = values.ndim - 3
    length = values.shape[dimension]
    last_node = lax.slice_in_dim(values, length - 1, length, axis=dimension)
    arrived = passed_along(last_node, "py", 1)
    first_node = lax.slice_in_dim(values, 0, 1, axis=dimension) + arrived
    return jnp.concatenate(
        [first_node, lax.slice_in_dim(values, 1, length - 1, axis=dimension)], axis=dimension
    )


def spread(totals):
    return totals.reshape(3, 1, 1, 1, 1)


def energy_sum(residual, precond):
    return lax.psum(jnp.sum(residual * precond, axis=(1, 2, 3, 4)), ("px", "py"))


def body(forcing, initial_guess, forward_velocity, free_mask):
    free_float = free_mask.astype(jnp.float32)
    speed_sq = jnp.sum(jnp.square(forward_velocity.astype(jnp.float32)), axis=0)
    viscosity = VISC_BASE + VISC_GAIN * speed_sq
    weight_x = line_weights(free_mask.shape[0])[:, None, None, None]
    weight_y = line_weights(free_mask.shape[1])[:, None, None]
    weight_z = line_weights(7)[:, None]
    coef_x = viscosity * weight_y * weight_z
    coef_y = viscosity * weight_x * weight_z
    coef_z = viscosity * weight_x * weight_y
    mass_diag = weight_x * weight_y * weight_z * jnp.ones((free_mask.shape[3],), jnp.float32)
    coef_x_ext = extend_x(coef_x)
    coef_y_ext = extend_y(coef_y)
    diag_x = reduce_x(diag_term(coef_x_ext, 4))
    diag_y = reduce_y(diag_term(coef_y_ext, 3))
    diag_z = z_fold(diag_kernel(z_view(coef_z), 1))
    diagonal = diag_x + diag_y + diag_z + HELMHOLTZ * mass_diag
    coef_z_view = z_view(coef_z)

    def operate(values):
        term_x = reduce_x(direction_term(extend_x(values), coef_x_ext, 4))
        term_y = reduce_y(direction_term(extend_y(values), coef_y_ext, 3))
        term_z = z_fold(kernel(z_view(values), coef_z_view, 1))
        return free_float * (term_x + term_y + term_z + HELMHOLTZ * mass_diag * values)

    right_side = free_float * mass_diag * forcing
    solution = initial_guess
    residual = right_side - operate(initial_guess)
    precond = residual / diagonal
    energy_now = energy_sum(residual, precond)
    direction = precond
    for iteration in range(ITERS):
        applied = operate(direction)
        curvature = lax.psum(jnp.sum(direction * applied, axis=(1, 2, 3, 4)), ("px", "py"))
        step_length = spread(energy_now / curvature)
        solution = solution + step_length * direction
        residual = residual - step_length * applied
        precond = residual / diagonal
        energy_next = energy_sum(residual, precond)
        direction = precond + spread(energy_next / energy_now) * direction
        energy_now = energy_next
    return (solution, direction)


def solution(mesh):
    placed = (
        P(None, "px", "py", None, None),
        P(None, "px", "py", None, None),
        P(None, "px", "py", None, None),
        P("px", "py", None, None),
    )
    return jax.shard_map(
        body,
        mesh=mesh,
        in_specs=placed,
        out_specs=(P(None, "px", "py", None, None), P(None, "px", "py", None, None)),
        check_vma=False,
    )
```

profile of v0, /device:TPU:1, one launch (start us, length us, event | category | flops | bytes accessed | tf_op | source)
XLA Modules:
  0.0 393.7 jit_solution(17573299616021403080)
XLA Ops:
  0.6 1.1 multiply_reduce_fusion.5
  1.9 1.3 collective-permute-start.4
  3.2 0.6 slice.324
  3.8 3.2 collective-permute-start.1
  7.0 0.7 copy.257
  7.7 2.9 collective-permute-start
  10.6 0.7 copy.258
  11.3 1.3 collective-permute-start.3
  12.7 0.7 copy-done.12
  13.5 0.5 copy-done.10
  14.1 0.3 fusion.54
  15.1 0.6 copy-done.7
  15.7 0.7 fusion.2
  16.4 0.7 fusion.52
  17.6 0.7 copy-done.8
  19.0 0.9 maximum_multiply_fusion
  19.9 0.3 fusion.53
  20.3 4.8 %collective-permute-start.7 = (f32[7,1,7,128]{3,0,2,1:T(8,128)S(1)}, f32[7,1,7,128]{3,0,2,1:T(8,128)S(1)}, u32[]{:S(2)}, u32[]{:S(2)}) collective-permute-start(f32[7,1,7,128]{3,0,2,1:T(8,128)S(1)} %pad_add_fusion.14), channel_id=1, source_target_pairs={{0,1},{1,2},{2,3},{3,4},{4,5},{5,6},{6,7},{8,9},{9,10},{10,11},{11... | collective-permute-start | bytes 75272 | tf_op jit(solution)/shard_map/ppermute | solution.py:21
  25.2 0.8 maximum_multiply_fusion.2
  26.0 0.3 convolution_bitcast_fusion.12
  26.6 1.8 collective-permute-done.6
  28.6 1.6 fusion.4
  30.2 0.7 convolution_bitcast_fusion.10
  31.2 1.5 collective-permute-start.2
  32.8 0.7 fusion.6
  33.6 0.7 fusion.51
  34.5 3.7 collective-permute-start.5
  38.6 1.0 collective-permute-done.5
  39.6 0.5 broadcast_divide_fusion
  40.5 0.7 fusion.1
  41.2 0.7 fusion.56
  42.1 6.1 %collective-permute-start.8 = (f32[3,1,7,7,128]{4,1,3,2,0:T(1,128)S(1)}, f32[3,1,7,7,128]{4,1,3,2,0:T(1,128)S(1)}, u32[]{:S(2)}, u32[]{:S(2)}) collective-permute-start(f32[3,1,7,7,128]{4,1,3,2,0:T(1,128)S(1)} %slice.347), channel_id=1, source_target_pairs={{0,248},{8,0},{16,8},{24,16},{32,24},{40,32},{48,40},{56,48},{64,5... | collective-permute-start | bytes 225800 | tf_op jit(solution)/shard_map/ppermute | solution.py:15
  48.2 1.3 collective-permute-start.10
  49.6 0.7 fusion.8
  50.3 0.7 convolution_bitcast_fusion.6
  51.6 2.1 collective-permute-done.10
  53.7 0.7 fusion.10
  54.4 0.7 fusion.55
  55.5 4.1 %collective-permute-start.11 = (f32[3,7,1,7,128]{4,1,3,2,0:T(8,128)S(1)}, f32[3,7,1,7,128]{4,1,3,2,0:T(8,128)S(1)}, u32[]{:S(2)}, u32[]{:S(2)}) collective-permute-start(f32[3,7,1,7,128]{4,1,3,2,0:T(8,128)S(1)} %pad_add_fusion.9), channel_id=1, source_target_pairs={{0,1},{1,2},{2,3},{3,4},{4,5},{5,6},{6,7},{8,9},{9,10},{10,11},{11... | collective-permute-start | bytes 225800 | tf_op jit(solution)/shard_map/ppermute | solution.py:21
  59.7 1.0 collective-permute-done.9
  61.1 0.5 multiply_reduce_fusion.3
  61.7 84.8 %all-reduce.24 = (f32[3]{0:T(128)S(1)}, f32[3]{0:T(128)S(1)}) all-reduce(f32[3]{0:T(128)S(1)} %get-tuple-element.11, f32[3]{0:T(128)S(1)} %get-tuple-element.10), channel_id=1, replica_groups=mesh['px'=32,'py'=8] {'px','py'}, use_global_device_ids=true, to_apply=%region_2.3 | all-reduce | flops 6 | bytes 48 | tf_op jit(solution)/shard_map/psum | solution.py:200
  146.5 0.3 multiply_reduce_fusion.2
  146.8 74.6 %psum.37 = f32[3]{0:T(128)S(1)} all-reduce(f32[3]{0:T(128)S(1)} %get-tuple-element.16), channel_id=1, replica_groups=mesh['px'=32,'py'=8] {'px','py'}, use_global_device_ids=true, to_apply=%region_6.7 | all-reduce | flops 3 | bytes 24 | tf_op jit(solution)/shard_map/psum | solution.py:200
  221.9 0.8 copy-done.2
  222.7 0.7 fusion
  223.4 0.7 fusion.58
  224.3 0.8 collective-permute-start.12
  225.0 1.3 collective-permute-start.14
  226.5 1.7 collective-permute-done.12
  228.1 0.7 fusion.12
  228.9 0.7 convolution_bitcast_fusion.2
  230.3 0.9 copy-done.4
  231.2 0.7 fusion.14
  231.9 0.7 fusion.57
  232.7 2.3 collective-permute-start.13
  235.1 1.8 collective-permute-start.15
  237.2 1.7 collective-permute-done.15
  239.0 0.5 multiply_reduce_fusion.1
  239.4 78.2 %psum.38 = f32[3]{0:T(128)S(1)} all-reduce(f32[3]{0:T(128)S(1)} %get-tuple-element.14), channel_id=1, replica_groups=mesh['px'=32,'py'=8] {'px','py'}, use_global_device_ids=true, to_apply=%region_8.9 | all-reduce | flops 3 | bytes 24 | tf_op jit(solution)/shard_map/psum | solution.py:236
  317.9 73.5 %psum.39 = f32[3]{0:T(128)S(1)} all-reduce(f32[3]{0:T(128)S(1)} %multiply_reduce_fusion), channel_id=1, replica_groups=mesh['px'=32,'py'=8] {'px','py'}, use_global_device_ids=true, to_apply=%region_10.11 | all-reduce | flops 3 | bytes 24 | tf_op jit(solution)/shard_map/psum | solution.py:200
  391.4 0.4 multiply_add_fusion
  391.8 0.9 copy.203
  392.8 0.9 copy.204
  (145 shorter events, 8.0 us)
Async XLA Ops:
  0.6 1.1 copy-start.11
  1.9 17.1 %collective-permute-start.4 = (f32[7,1,7,128]{3,0,2,1:T(8,128)S(1)}, f32[7,1,7,128]{3,0,2,1:T(8,128)}, u32[]{:S(2)}, u32[]{:S(2)}) collective-permute-start(f32[7,1,7,128]{3,0,2,1:T(8,128)S(1)} %slice.328), channel_id=1, source_target_pairs={{1,0},{2,1},{3,2},{4,3},{5,4},{6,5},{7,6},{9,8},{10,9},{11,10},{12... | collective-permute-start | bytes 75272 | tf_op jit(solution)/shard_map/ppermute | solution.py:21
  3.8 3.2 slice-start
  3.8 21.4 %collective-permute-start.1 = (f32[1,7,7,128]{3,0,2,1:T(1,128)}, f32[1,7,7,128]{3,0,2,1:T(1,128)}, u32[]{:S(2)}, u32[]{:S(2)}) collective-permute-start(f32[1,7,7,128]{3,0,2,1:T(1,128)} %slice.324), channel_id=1, source_target_pairs={{0,248},{8,0},{16,8},{24,16},{32,24},{40,32},{48,40},{56,48},{64,5... | collective-permute-start | bytes 75272 | tf_op jit(solution)/shard_map/ppermute | solution.py:15
  7.7 2.9 slice-start.1
  7.7 20.9 %collective-permute-start = (f32[3,1,7,7,128]{4,1,3,2,0:T(1,128)}, f32[3,1,7,7,128]{4,1,3,2,0:T(1,128)}, u32[]{:S(2)}, u32[]{:S(2)}) collective-permute-start(f32[3,1,7,7,128]{4,1,3,2,0:T(1,128)} %copy.257), channel_id=1, source_target_pairs={{0,248},{8,0},{16,8},{24,16},{32,24},{40,32},{48,40},{56,48},{64,5... | collective-permute-start | bytes 225800 | tf_op jit(solution)/shard_map/ppermute | solution.py:15
  11.3 21.5 %collective-permute-start.3 = (f32[3,7,1,7,128]{4,2,3,1,0:T(1,128)}, f32[3,7,1,7,128]{4,2,3,1,0:T(1,128)S(1)}, u32[]{:S(2)}, u32[]{:S(2)}) collective-permute-start(f32[3,7,1,7,128]{4,2,3,1,0:T(1,128)} %copy.258), channel_id=1, source_target_pairs={{1,0},{2,1},{3,2},{4,3},{5,4},{6,5},{7,6},{9,8},{10,9},{11,10},{12... | collective-permute-start | bytes 225800 | tf_op jit(solution)/shard_map/ppermute | solution.py:21
  12.7 0.7 copy-start.12
  13.4 0.7 copy-start.10
  13.5 1.1 copy-start
  14.0 26.4 %copy-start.1 = (f32[7,7,8,128]{3,2,1,0:T(8,128)}, f32[7,7,8,128]{3,2,1,0:T(8,128)S(1)}, u32[]{:S(2)}) copy-start(f32[7,7,8,128]{3,2,1,0:T(8,128)S(1)} %copy.176) | copy-start | bytes 602116
  15.0 0.7 copy-start.7
  17.4 0.9 copy-start.8
  18.9 42.2 %copy-start.5 = (f32[7,7,7,128]{3,0,2,1:T(8,128)}, f32[7,7,7,128]{3,0,2,1:T(8,128)S(1)}, u32[]{:S(2)}) copy-start(f32[7,7,7,128]{3,0,2,1:T(8,128)S(1)} %copy.162) | copy-start | bytes 526852
  19.9 33.9 %copy-start.3 = (f32[7,8,7,128]{3,1,2,0:T(8,128)}, f32[7,8,7,128]{3,1,2,0:T(8,128)S(1)}, u32[]{:S(2)}) copy-start(f32[7,8,7,128]{3,1,2,0:T(8,128)S(1)} %copy.170) | copy-start | bytes 602116
  20.3 6.2 %collective-permute-start.7 = (f32[7,1,7,128]{3,0,2,1:T(8,128)S(1)}, f32[7,1,7,128]{3,0,2,1:T(8,128)S(1)}, u32[]{:S(2)}, u32[]{:S(2)}) collective-permute-start(f32[7,1,7,128]{3,0,2,1:T(8,128)S(1)} %pad_add_fusion.14), channel_id=1, source_target_pairs={{0,1},{1,2},{2,3},{3,4},{4,5},{5,6},{6,7},{8,9},{9,10},{10,11},{11... | collective-permute-start | bytes 75272 | tf_op jit(solution)/shard_map/ppermute | solution.py:21
  26.5 1.9 collective-permute-start.6
  31.2 7.1 %collective-permute-start.2 = (f32[3,1,7,7,128]{4,1,3,2,0:T(1,128)S(1)}, f32[3,1,7,7,128]{4,1,3,2,0:T(1,128)S(1)}, u32[]{:S(2)}, u32[]{:S(2)}) collective-permute-start(f32[3,1,7,7,128]{4,1,3,2,0:T(1,128)S(1)} %pad_add_fusion.13), channel_id=1, source_target_pairs={{0,8},{8,16},{16,24},{24,32},{32,40},{40,48},{48,56},{56,64},{64,7... | collective-permute-start | bytes 225800 | tf_op jit(solution)/shard_map/ppermute | solution.py:15
  34.5 5.1 %collective-permute-start.5 = (f32[3,7,1,7,128]{4,1,3,2,0:T(8,128)S(1)}, f32[3,7,1,7,128]{4,1,3,2,0:T(8,128)S(1)}, u32[]{:S(2)}, u32[]{:S(2)}) collective-permute-start(f32[3,7,1,7,128]{4,1,3,2,0:T(8,128)S(1)} %pad_add_fusion.10), channel_id=1, source_target_pairs={{0,1},{1,2},{2,3},{3,4},{4,5},{5,6},{6,7},{8,9},{9,10},{10,11},{11... | collective-permute-start | bytes 225800 | tf_op jit(solution)/shard_map/ppermute | solution.py:21
  38.5 1.1 copy-start.9
  42.1 7.5 %collective-permute-start.8 = (f32[3,1,7,7,128]{4,1,3,2,0:T(1,128)S(1)}, f32[3,1,7,7,128]{4,1,3,2,0:T(1,128)S(1)}, u32[]{:S(2)}, u32[]{:S(2)}) collective-permute-start(f32[3,1,7,7,128]{4,1,3,2,0:T(1,128)S(1)} %slice.347), channel_id=1, source_target_pairs={{0,248},{8,0},{16,8},{24,16},{32,24},{40,32},{48,40},{56,48},{64,5... | collective-permute-start | bytes 225800 | tf_op jit(solution)/shard_map/ppermute | solution.py:15
  48.2 5.5 %collective-permute-start.10 = (f32[3,7,1,7,128]{4,1,3,2,0:T(8,128)S(1)}, f32[3,7,1,7,128]{4,1,3,2,0:T(8,128)S(1)}, u32[]{:S(2)}, u32[]{:S(2)}) collective-permute-start(f32[3,7,1,7,128]{4,1,3,2,0:T(8,128)S(1)} %slice.350), channel_id=1, source_target_pairs={{1,0},{2,1},{3,2},{4,3},{5,4},{6,5},{7,6},{9,8},{10,9},{11,10},{12... | collective-permute-start | bytes 225800 | tf_op jit(solution)/shard_map/ppermute | solution.py:21
  55.3 5.4 %collective-permute-start.9 = (f32[3,1,7,7,128]{4,1,3,2,0:T(1,128)S(1)}, f32[3,1,7,7,128]{4,1,3,2,0:T(1,128)S(1)}, u32[]{:S(2)}, u32[]{:S(2)}) collective-permute-start(f32[3,1,7,7,128]{4,1,3,2,0:T(1,128)S(1)} %pad_add_fusion.12), channel_id=1, source_target_pairs={{0,8},{8,16},{16,24},{24,32},{32,40},{40,48},{48,56},{56,64},{64,7... | collective-permute-start | bytes 225800 | tf_op jit(solution)/shard_map/ppermute | solution.py:15
  55.5 5.6 %collective-permute-start.11 = (f32[3,7,1,7,128]{4,1,3,2,0:T(8,128)S(1)}, f32[3,7,1,7,128]{4,1,3,2,0:T(8,128)S(1)}, u32[]{:S(2)}, u32[]{:S(2)}) collective-permute-start(f32[3,7,1,7,128]{4,1,3,2,0:T(8,128)S(1)} %pad_add_fusion.9), channel_id=1, source_target_pairs={{0,1},{1,2},{2,3},{3,4},{4,5},{5,6},{6,7},{8,9},{9,10},{10,11},{11... | collective-permute-start | bytes 225800 | tf_op jit(solution)/shard_map/ppermute | solution.py:21
  221.7 0.9 copy-start.2
  224.3 3.9 collective-permute-start.12
  225.0 5.2 %collective-permute-start.14 = (f32[3,7,1,7,128]{4,1,3,2,0:T(8,128)S(1)}, f32[3,7,1,7,128]{4,1,3,2,0:T(8,128)S(1)}, u32[]{:S(2)}, u32[]{:S(2)}) collective-permute-start(f32[3,7,1,7,128]{4,1,3,2,0:T(8,128)S(1)} %slice.362), channel_id=1, source_target_pairs={{1,0},{2,1},{3,2},{4,3},{5,4},{6,5},{7,6},{9,8},{10,9},{11,10},{12... | collective-permute-start | bytes 225800 | tf_op jit(solution)/shard_map/ppermute | solution.py:21
  230.2 0.9 copy-start.4
  232.7 4.3 %collective-permute-start.13 = (f32[3,1,7,7,128]{4,1,3,2,0:T(1,128)S(1)}, f32[3,1,7,7,128]{4,1,3,2,0:T(1,128)S(1)}, u32[]{:S(2)}, u32[]{:S(2)}) collective-permute-start(f32[3,1,7,7,128]{4,1,3,2,0:T(1,128)S(1)} %pad_add_fusion.11), channel_id=1, source_target_pairs={{0,8},{8,16},{16,24},{24,32},{32,40},{40,48},{48,56},{56,64},{64,7... | collective-permute-start | bytes 225800 | tf_op jit(solution)/shard_map/ppermute | solution.py:15
  235.1 3.8 collective-permute-start.15
  237.2 1.7 copy-start.6
where the time goes:
time: 395 us; the launch traced here: 394 us
  blocking collectives  311 us (79%)
  starting transfers between devices  36.5 us (9%)
  matrix products  14.2 us (4%)
  local copies, waits for them, and re-layouts  11.6 us (3%)
  waiting for transfers between devices  9.8 us (2%)
  other arithmetic  8.82 us (2%)
    psum x3, blocking collectives, energy_sum(): lax.psum(jnp.sum(residual * precond, axis=(1, 2, 3, 4)), ('px', 'py'))  233 us
    psum x1, blocking collectives, body(): lax.psum(jnp.sum(direction * applied, axis=(1, 2, 3, 4)), ('px', 'py'))  78.2 us
    ppermute x8, starting transfers between devices, passed_along(): return lax.ppermute(block, axis, route)  19.6 us
    ppermute x8, starting transfers between devices, shifted(): lax.ppermute(value, axis, [(i, (i + by) % count) for i in range(count)])  16.9 us
  transfers between devices with their start and end apart: 16, of which 8 were waited for; matrix products, arithmetic and copies ran while one was open for 5% of the time, Pallas kernels for 0%

commit v1 on v0

--- a/solution.py
+++ b/solution.py
@@ -233,7 +233,9 @@
     direction = precond
     for iteration in range(ITERS):
         applied = operate(direction)
-        curvature = lax.psum(jnp.sum(direction * applied, axis=(1, 2, 3, 4)), ("px", "py"))
+        curvature = jnp.sum(direction * applied, axis=(1, 2, 3, 4))
+        for mesh_axis in ("px", "py"):
+            curvature = lax.psum(curvature, mesh_axis)
         step_length = spread(energy_now / curvature)
         solution = solution + step_length * direction
         residual = residual - step_length * applied

time: 395 us -> 477 us (1.21)
  blocking collectives: 311 us -> 392 us
    psum x1 -> x4, blocking collectives: 78.2 us -> 162 us  [body(): curvature = lax.psum(curvature, mesh_axis)]
  transfers between devices with their start and end apart: 16 -> 16, of which waited for: 8 -> 8; matrix products, arithmetic and copies ran while one was open for 5% -> 4% of each run, Pallas kernels for 0% -> 0%
where the time goes in v1:
time: 477 us; the launch traced here: 476 us
  blocking collectives  392 us (82%)
  starting transfers between devices  38.4 us (8%)
  matrix products  14.2 us (3%)
  local copies, waits for them, and re-layouts  11.6 us (2%)
  waiting for transfers between devices  9.69 us (2%)
  other arithmetic  8.82 us (2%)
    psum x3, blocking collectives, energy_sum(): lax.psum(jnp.sum(residual * precond, axis=(1, 2, 3, 4)), ('px', 'py'))  230 us
    psum x4, blocking collectives, body(): curvature = lax.psum(curvature, mesh_axis)  162 us
    ppermute x8, starting transfers between devices, passed_along(): return lax.ppermute(block, axis, route)  21.1 us
    ppermute x8, starting transfers between devices, shifted(): lax.ppermute(value, axis, [(i, (i + by) % count) for i in range(count)])  17.3 us
  transfers between devices with their start and end apart: 16, of which 8 were waited for; matrix products, arithmetic and copies ran while one was open for 4% of the time, Pallas kernels for 0%

profile of v1, /device:TPU:1, one launch (start us, length us, event | category | flops | bytes accessed | tf_op | source)
XLA Modules:
  0.0 476.5 jit_solution(13043440396178364491)
XLA Ops:
  0.6 1.1 multiply_reduce_fusion.5
  1.9 1.3 collective-permute-start.4
  3.2 0.6 slice.324
  3.8 3.2 collective-permute-start.1
  7.0 0.7 copy.257
  7.7 2.9 collective-permute-start
  10.6 0.7 copy.258
  11.4 1.3 collective-permute-start.3
  12.7 0.7 copy-done.12
  13.6 0.5 copy-done.10
  15.1 0.6 copy-done.7
  15.7 0.7 fusion.2
  16.4 0.7 fusion.52
  17.7 0.7 copy-done.8
  19.0 0.9 maximum_multiply_fusion
  20.4 4.8 %collective-permute-start.7 = (f32[7,1,7,128]{3,0,2,1:T(8,128)S(1)}, f32[7,1,7,128]{3,0,2,1:T(8,128)S(1)}, u32[]{:S(2)}, u32[]{:S(2)}) collective-permute-start(f32[7,1,7,128]{3,0,2,1:T(8,128)S(1)} %pad_add_fusion.14), channel_id=1, source_target_pairs={{0,1},{1,2},{2,3},{3,4},{4,5},{5,6},{6,7},{8,9},{9,10},{10,11},{11... | collective-permute-start | bytes 75272 | tf_op jit(solution)/shard_map/ppermute | solution.py:21
  25.2 0.8 maximum_multiply_fusion.2
  26.6 1.8 collective-permute-done.6
  28.6 1.6 fusion.4
  30.3 0.7 convolution_bitcast_fusion.10
  31.3 1.5 collective-permute-start.2
  32.9 0.7 fusion.6
  33.6 0.7 fusion.51
  34.5 3.7 collective-permute-start.5
  38.6 1.0 collective-permute-done.5
  39.7 0.5 broadcast_divide_fusion
  40.5 0.7 fusion.1
  41.2 0.7 fusion.56
  42.1 6.0 %collective-permute-start.8 = (f32[3,1,7,7,128]{4,1,3,2,0:T(1,128)S(1)}, f32[3,1,7,7,128]{4,1,3,2,0:T(1,128)S(1)}, u32[]{:S(2)}, u32[]{:S(2)}) collective-permute-start(f32[3,1,7,7,128]{4,1,3,2,0:T(1,128)S(1)} %slice.347), channel_id=1, source_target_pairs={{0,248},{8,0},{16,8},{24,16},{32,24},{40,32},{48,40},{56,48},{64,5... | collective-permute-start | bytes 225800 | tf_op jit(solution)/shard_map/ppermute | solution.py:15
  48.2 1.3 collective-permute-start.10
  49.6 0.7 fusion.8
  50.4 0.7 convolution_bitcast_fusion.6
  51.6 2.1 collective-permute-done.10
  53.8 0.7 fusion.10
  54.5 0.7 fusion.55
  55.5 4.1 collective-permute-start.11
  59.7 1.0 collective-permute-done.9
  61.1 0.5 multiply_reduce_fusion.3
  61.7 68.2 %psum.50 = f32[3]{0:T(128)S(1)} all-reduce(f32[3]{0:T(128)S(1)} %get-tuple-element.10), channel_id=1, replica_groups=mesh['px'=32,'py'=8] {'px'}, use_global_device_ids=true, to_apply=%region_4.5 | all-reduce | flops 3 | bytes 24 | tf_op jit(solution)/shard_map/psum | solution.py:238
  129.9 16.2 %psum.51 = f32[3]{0:T(128)S(1)} all-reduce(f32[3]{0:T(128)S(1)} %psum.50), channel_id=1, replica_groups=mesh['px'=32,'py'=8] {'py'}, use_global_device_ids=true, to_apply=%region_5.6 | all-reduce | flops 3 | bytes 24 | tf_op jit(solution)/shard_map/psum | solution.py:238
  146.1 79.0 %psum.49 = f32[3]{0:T(128)S(1)} all-reduce(f32[3]{0:T(128)S(1)} %get-tuple-element.11), channel_id=1, replica_groups=mesh['px'=32,'py'=8] {'px','py'}, use_global_device_ids=true, to_apply=%region_2.3 | all-reduce | flops 3 | bytes 24 | tf_op jit(solution)/shard_map/psum | solution.py:200
  225.5 73.9 %psum.52 = f32[3]{0:T(128)S(1)} all-reduce(f32[3]{0:T(128)S(1)} %get-tuple-element.14), channel_id=1, replica_groups=mesh['px'=32,'py'=8] {'px','py'}, use_global_device_ids=true, to_apply=%region_7.8 | all-reduce | flops 3 | bytes 24 | tf_op jit(solution)/shard_map/psum | solution.py:200
  299.8 0.8 copy-done.2
  300.6 0.7 fusion
  301.3 0.7 fusion.58
  302.2 0.8 collective-permute-start.12
  303.0 1.3 collective-permute-start.14
  304.4 1.7 collective-permute-done.12
  306.1 0.7 fusion.12
  306.8 0.7 convolution_bitcast_fusion.2
  308.0 0.4 collective-permute-done.14
  308.4 0.9 copy-done.4
  309.3 0.7 fusion.14
  310.0 0.7 fusion.57
  310.9 2.7 collective-permute-start.13
  313.6 3.4 collective-permute-start.15
  317.3 1.4 collective-permute-done.15
  318.7 0.5 multiply_reduce_fusion.1
  319.2 65.0 %psum.53 = f32[3]{0:T(128)S(1)} all-reduce(f32[3]{0:T(128)S(1)} %get-tuple-element.12), channel_id=1, replica_groups=mesh['px'=32,'py'=8] {'px'}, use_global_device_ids=true, to_apply=%region_9.10 | all-reduce | flops 3 | bytes 24 | tf_op jit(solution)/shard_map/psum | solution.py:238
  384.2 12.3 %psum.54 = f32[3]{0:T(128)S(1)} all-reduce(f32[3]{0:T(128)S(1)} %psum.53), channel_id=1, replica_groups=mesh['px'=32,'py'=8] {'py'}, use_global_device_ids=true, to_apply=%region_10.11 | all-reduce | flops 3 | bytes 24 | tf_op jit(solution)/shard_map/psum | solution.py:238
  396.8 77.4 %psum.55 = f32[3]{0:T(128)S(1)} all-reduce(f32[3]{0:T(128)S(1)} %multiply_reduce_fusion), channel_id=1, replica_groups=mesh['px'=32,'py'=8] {'px','py'}, use_global_device_ids=true, to_apply=%region_12.13 | all-reduce | flops 3 | bytes 24 | tf_op jit(solution)/shard_map/psum | solution.py:200
  474.2 0.4 multiply_add_fusion
  474.6 0.9 copy.203
  475.5 0.9 copy.204
  (148 shorter events, 9.0 us)
Async XLA Ops:
  0.6 1.1 copy-start.11
  1.9 17.1 %collective-permute-start.4 = (f32[7,1,7,128]{3,0,2,1:T(8,128)S(1)}, f32[7,1,7,128]{3,0,2,1:T(8,128)}, u32[]{:S(2)}, u32[]{:S(2)}) collective-permute-start(f32[7,1,7,128]{3,0,2,1:T(8,128)S(1)} %slice.328), channel_id=1, source_target_pairs={{1,0},{2,1},{3,2},{4,3},{5,4},{6,5},{7,6},{9,8},{10,9},{11,10},{12... | collective-permute-start | bytes 75272 | tf_op jit(solution)/shard_map/ppermute | solution.py:21
  3.8 3.2 slice-start
  3.8 21.4 %collective-permute-start.1 = (f32[1,7,7,128]{3,0,2,1:T(1,128)}, f32[1,7,7,128]{3,0,2,1:T(1,128)}, u32[]{:S(2)}, u32[]{:S(2)}) collective-permute-start(f32[1,7,7,128]{3,0,2,1:T(1,128)} %slice.324), channel_id=1, source_target_pairs={{0,248},{8,0},{16,8},{24,16},{32,24},{40,32},{48,40},{56,48},{64,5... | collective-permute-start | bytes 75272 | tf_op jit(solution)/shard_map/ppermute | solution.py:15
  7.7 2.9 slice-start.1
  7.7 20.9 %collective-permute-start = (f32[3,1,7,7,128]{4,1,3,2,0:T(1,128)}, f32[3,1,7,7,128]{4,1,3,2,0:T(1,128)}, u32[]{:S(2)}, u32[]{:S(2)}) collective-permute-start(f32[3,1,7,7,128]{4,1,3,2,0:T(1,128)} %copy.257), channel_id=1, source_target_pairs={{0,248},{8,0},{16,8},{24,16},{32,24},{40,32},{48,40},{56,48},{64,5... | collective-permute-start | bytes 225800 | tf_op jit(solution)/shard_map/ppermute | solution.py:15
  11.4 21.5 %collective-permute-start.3 = (f32[3,7,1,7,128]{4,2,3,1,0:T(1,128)}, f32[3,7,1,7,128]{4,2,3,1,0:T(1,128)S(1)}, u32[]{:S(2)}, u32[]{:S(2)}) collective-permute-start(f32[3,7,1,7,128]{4,2,3,1,0:T(1,128)} %copy.258), channel_id=1, source_target_pairs={{1,0},{2,1},{3,2},{4,3},{5,4},{6,5},{7,6},{9,8},{10,9},{11,10},{12... | collective-permute-start | bytes 225800 | tf_op jit(solution)/shard_map/ppermute | solution.py:21
  12.7 0.7 copy-start.12
  13.4 0.7 copy-start.10
  13.5 1.1 copy-start
  14.1 26.4 %copy-start.1 = (f32[7,7,8,128]{3,2,1,0:T(8,128)}, f32[7,7,8,128]{3,2,1,0:T(8,128)S(1)}, u32[]{:S(2)}) copy-start(f32[7,7,8,128]{3,2,1,0:T(8,128)S(1)} %copy.176) | copy-start | bytes 602116
  15.0 0.7 copy-start.7
  17.4 0.9 copy-start.8
  18.9 42.2 %copy-start.5 = (f32[7,7,7,128]{3,0,2,1:T(8,128)}, f32[7,7,7,128]{3,0,2,1:T(8,128)S(1)}, u32[]{:S(2)}) copy-start(f32[7,7,7,128]{3,0,2,1:T(8,128)S(1)} %copy.162) | copy-start | bytes 526852
  19.9 33.9 %copy-start.3 = (f32[7,8,7,128]{3,1,2,0:T(8,128)}, f32[7,8,7,128]{3,1,2,0:T(8,128)S(1)}, u32[]{:S(2)}) copy-start(f32[7,8,7,128]{3,1,2,0:T(8,128)S(1)} %copy.170) | copy-start | bytes 602116
  20.4 6.2 %collective-permute-start.7 = (f32[7,1,7,128]{3,0,2,1:T(8,128)S(1)}, f32[7,1,7,128]{3,0,2,1:T(8,128)S(1)}, u32[]{:S(2)}, u32[]{:S(2)}) collective-permute-start(f32[7,1,7,128]{3,0,2,1:T(8,128)S(1)} %pad_add_fusion.14), channel_id=1, source_target_pairs={{0,1},{1,2},{2,3},{3,4},{4,5},{5,6},{6,7},{8,9},{9,10},{10,11},{11... | collective-permute-start | bytes 75272 | tf_op jit(solution)/shard_map/ppermute | solution.py:21
  26.5 1.9 collective-permute-start.6
  31.3 7.1 %collective-permute-start.2 = (f32[3,1,7,7,128]{4,1,3,2,0:T(1,128)S(1)}, f32[3,1,7,7,128]{4,1,3,2,0:T(1,128)S(1)}, u32[]{:S(2)}, u32[]{:S(2)}) collective-permute-start(f32[3,1,7,7,128]{4,1,3,2,0:T(1,128)S(1)} %pad_add_fusion.13), channel_id=1, source_target_pairs={{0,8},{8,16},{16,24},{24,32},{32,40},{40,48},{48,56},{56,64},{64,7... | collective-permute-start | bytes 225800 | tf_op jit(solution)/shard_map/ppermute | solution.py:15
  34.5 5.1 %collective-permute-start.5 = (f32[3,7,1,7,128]{4,1,3,2,0:T(8,128)S(1)}, f32[3,7,1,7,128]{4,1,3,2,0:T(8,128)S(1)}, u32[]{:S(2)}, u32[]{:S(2)}) collective-permute-start(f32[3,7,1,7,128]{4,1,3,2,0:T(8,128)S(1)} %pad_add_fusion.10), channel_id=1, source_target_pairs={{0,1},{1,2},{2,3},{3,4},{4,5},{5,6},{6,7},{8,9},{9,10},{10,11},{11... | collective-permute-start | bytes 225800 | tf_op jit(solution)/shard_map/ppermute | solution.py:21
  38.6 1.1 copy-start.9
  42.1 7.5 %collective-permute-start.8 = (f32[3,1,7,7,128]{4,1,3,2,0:T(1,128)S(1)}, f32[3,1,7,7,128]{4,1,3,2,0:T(1,128)S(1)}, u32[]{:S(2)}, u32[]{:S(2)}) collective-permute-start(f32[3,1,7,7,128]{4,1,3,2,0:T(1,128)S(1)} %slice.347), channel_id=1, source_target_pairs={{0,248},{8,0},{16,8},{24,16},{32,24},{40,32},{48,40},{56,48},{64,5... | collective-permute-start | bytes 225800 | tf_op jit(solution)/shard_map/ppermute | solution.py:15
  48.2 5.5 %collective-permute-start.10 = (f32[3,7,1,7,128]{4,1,3,2,0:T(8,128)S(1)}, f32[3,7,1,7,128]{4,1,3,2,0:T(8,128)S(1)}, u32[]{:S(2)}, u32[]{:S(2)}) collective-permute-start(f32[3,7,1,7,128]{4,1,3,2,0:T(8,128)S(1)} %slice.350), channel_id=1, source_target_pairs={{1,0},{2,1},{3,2},{4,3},{5,4},{6,5},{7,6},{9,8},{10,9},{11,10},{12... | collective-permute-start | bytes 225800 | tf_op jit(solution)/shard_map/ppermute | solution.py:21
  55.4 5.4 %collective-permute-start.9 = (f32[3,1,7,7,128]{4,1,3,2,0:T(1,128)S(1)}, f32[3,1,7,7,128]{4,1,3,2,0:T(1,128)S(1)}, u32[]{:S(2)}, u32[]{:S(2)}) collective-permute-start(f32[3,1,7,7,128]{4,1,3,2,0:T(1,128)S(1)} %pad_add_fusion.12), channel_id=1, source_target_pairs={{0,8},{8,16},{16,24},{24,32},{32,40},{40,48},{48,56},{56,64},{64,7... | collective-permute-start | bytes 225800 | tf_op jit(solution)/shard_map/ppermute | solution.py:15
  55.5 5.6 %collective-permute-start.11 = (f32[3,7,1,7,128]{4,1,3,2,0:T(8,128)S(1)}, f32[3,7,1,7,128]{4,1,3,2,0:T(8,128)S(1)}, u32[]{:S(2)}, u32[]{:S(2)}) collective-permute-start(f32[3,7,1,7,128]{4,1,3,2,0:T(8,128)S(1)} %pad_add_fusion.9), channel_id=1, source_target_pairs={{0,1},{1,2},{2,3},{3,4},{4,5},{5,6},{6,7},{8,9},{9,10},{10,11},{11... | collective-permute-start | bytes 225800 | tf_op jit(solution)/shard_map/ppermute | solution.py:21
  299.7 0.9 copy-start.2
  302.2 3.9 collective-permute-start.12
  303.0 5.4 %collective-permute-start.14 = (f32[3,7,1,7,128]{4,1,3,2,0:T(8,128)S(1)}, f32[3,7,1,7,128]{4,1,3,2,0:T(8,128)S(1)}, u32[]{:S(2)}, u32[]{:S(2)}) collective-permute-start(f32[3,7,1,7,128]{4,1,3,2,0:T(8,128)S(1)} %slice.362), channel_id=1, source_target_pairs={{1,0},{2,1},{3,2},{4,3},{5,4},{6,5},{7,6},{9,8},{10,9},{11,10},{12... | collective-permute-start | bytes 225800 | tf_op jit(solution)/shard_map/ppermute | solution.py:21
  308.4 0.9 copy-start.4
  310.9 6.2 %collective-permute-start.13 = (f32[3,1,7,7,128]{4,1,3,2,0:T(1,128)S(1)}, f32[3,1,7,7,128]{4,1,3,2,0:T(1,128)S(1)}, u32[]{:S(2)}, u32[]{:S(2)}) collective-permute-start(f32[3,1,7,7,128]{4,1,3,2,0:T(1,128)S(1)} %pad_add_fusion.11), channel_id=1, source_target_pairs={{0,8},{8,16},{16,24},{24,32},{32,40},{40,48},{48,56},{56,64},{64,7... | collective-permute-start | bytes 225800 | tf_op jit(solution)/shard_map/ppermute | solution.py:15
  313.6 5.1 %collective-permute-start.15 = (f32[3,7,1,7,128]{4,1,3,2,0:T(8,128)S(1)}, f32[3,7,1,7,128]{4,1,3,2,0:T(8,128)S(1)}, u32[]{:S(2)}, u32[]{:S(2)}) collective-permute-start(f32[3,7,1,7,128]{4,1,3,2,0:T(8,128)S(1)} %pad_add_fusion.8), channel_id=1, source_target_pairs={{0,1},{1,2},{2,3},{3,4},{4,5},{5,6},{6,7},{8,9},{9,10},{10,11},{11... | collective-permute-start | bytes 225800 | tf_op jit(solution)/shard_map/ppermute | solution.py:21
  317.3 1.5 copy-start.6
